TPU v7x, 32 devices: a whole 2x2x4 slice. The times are simulated.
32 devices in a mesh: tm: 16 (over z, x, core), freq: 2 (over y).
Axes of the slice: x: 2, y: 2, z: 4, core: 2. Of those that a mesh axis runs over, the one named last changes fastest.
Arguments:
- visibilities: float32 [16, 2, 8, 512], P('tm', 'freq'), may hold values from -6 to 6
- coherency: bfloat16 [16, 2, 8, 64, 512], P('tm', 'freq'), may hold values from -0.75 to 0.75
- stations: int32 [16, 2, 512], P('tm'), may hold values from 0 to 511, as said below
- jones: float32 [2, 8, 32768], P('freq', None, 'tm'), may hold values from -3 to 3
- dual: float32 [2, 8, 32768], P('freq', None, 'tm'), may hold values from -1.8 to 1.8
- cluster: int32 [64], replicated, may hold values from 0 to 7
- rho_table: float32 [8], replicated, may hold values from 0.3 to 3
Outputs:
- jones_out: float32 [2, 8, 32768], P('freq', None, 'tm')
- dual_out: float32 [2, 8, 32768], P('freq', None, 'tm')
- consensus: float32 [1, 8, 32768], P(None, None, 'tm')
Inputs may be any that keep to these rules, and one draw needn't show every extreme that they name: Each baseline joins two different stations.
All inputs are finite; a program needn't handle non-finite values.
Results may differ from a plain program's by a relative error of at most 0.0003.
Values may be sent and summed in bfloat16 or wider, within the bound.
A program may use at most 64 MiB of HBM per device.

v0:
```python
import math

import jax
import jax.numpy as jnp
import numpy as np
from jax import lax
from jax.sharding import PartitionSpec as P

S = 512
K = 64
ITERS = 2


step_size = 0.5
epsilon = 1e-06
highest = lax.Precision.HIGHEST


def poly_basis(channels, degrees):
    points = np.linspace(-1.0, 1.0, channels)
    columns = []
    for degree in range(degrees):
        column = points**degree
        for earlier in columns:
            column = column - np.dot(earlier, column) * earlier
        column = column / np.sqrt(np.dot(column, column))
        columns.append(column)
    return np.stack(columns, axis=1).astype(np.float32)


def split_entries(stacked):
    return [
        [
            (
                stacked[4 * left_index + 2 * right_index],
                stacked[4 * left_index + 2 * right_index + 1],
            )
            for right_index in range(2)
        ]
        for left_index in range(2)
    ]


def times_pair(left_val, right_val):
    return (
        left_val[0] * right_val[0] - left_val[1] * right_val[1],
        left_val[0] * right_val[1] + left_val[1] * right_val[0],
    )


def times_conj(left_val, right_val):
    return (
        left_val[0] * right_val[0] + left_val[1] * right_val[1],
        left_val[1] * right_val[0] - left_val[0] * right_val[1],
    )


def add_pairs(left_val, right_val):
    return (left_val[0] + right_val[0], left_val[1] + right_val[1])


def direction_model(first_gain, sky_model, second_gain):
    first_mat = split_entries(first_gain)
    sky_mat = split_entries(sky_model)
    second_mat = split_entries(second_gain)
    product = [
        [
            add_pairs(
                times_pair(first_mat[left_index][0], sky_mat[0][right_index]),
                times_pair(first_mat[left_index][1], sky_mat[1][right_index]),
            )
            for right_index in range(2)
        ]
        for left_index in range(2)
    ]
    result = [
        [
            add_pairs(
                times_conj(product[left_index][0], second_mat[right_index][0]),
                times_conj(product[left_index][1], second_mat[right_index][1]),
            )
            for right_index in range(2)
        ]
        for left_index in range(2)
    ]
    components = []
    for left_index in range(2):
        for right_index in range(2):
            components.append(result[left_index][right_index][0])
            components.append(result[left_index][right_index][1])
    return jnp.stack(components, axis=0)


def model_sum(gain_block, first_station, second_station, sky_model):
    first_gain = jnp.take(gain_block, first_station, axis=2)
    second_gain = jnp.take(gain_block, second_station, axis=2)
    return jnp.sum(direction_model(first_gain, sky_model, second_gain), axis=1)


def body(visibilities, coherency, stations, jones, dual, cluster, rho_table):
    slot_count = lax.axis_size("tm")
    channels = lax.axis_size("freq")
    degrees = min(3, channels - 1)
    shard_len = jones.shape[2]
    local_dirs = shard_len // S
    tm_index = lax.axis_index("tm")
    freq_index = lax.axis_index("freq")
    weight = np.float32(math.sqrt(S / (2.0 * slot_count * visibilities.shape[3])))
    rho_dir = jnp.sum(
        jnp.where(
            cluster[:, None] == jnp.arange(rho_table.shape[0], dtype=jnp.int32)[None, :],
            rho_table[None, :],
            jnp.float32(0.0),
        ),
        axis=1,
    )
    rho_local = jnp.repeat(lax.dynamic_slice_in_dim(rho_dir, tm_index * local_dirs, local_dirs), S)
    poly_table = jnp.asarray(poly_basis(channels, degrees))
    basis_row = lax.dynamic_index_in_dim(poly_table, freq_index, 0, keepdims=False)

    def consensus_of(state, dual_now):
        poly_term = basis_row[:, None, None] * (state[0] + dual_now[0] / rho_local)
        return lax.psum(poly_term, "freq")

    def project(poly_coef):
        return jnp.sum(basis_row[:, None, None] * poly_coef, axis=0)[None]

    def state_gradient(current):
        gathered = lax.all_gather(current, "tm", axis=2, tiled=True)
        gain_block = gathered.reshape(8, K, S)
        first_st = stations[0, 0]
        second_st = stations[0, 1]
        sky_model = coherency[0, 0].astype(jnp.float32)
        model_vis, pullback = jax.vjp(
            lambda gains: model_sum(gains, first_st, second_st, sky_model), gain_block
        )
        grad_term = pullback(-weight * (visibilities[0, 0] - model_vis))[0]
        return lax.psum_scatter(
            grad_term.reshape(1, 8, K * S), "tm", scatter_dimension=2, tiled=True
        )

    current = jones
    dual_now = dual
    poly_coef = consensus_of(current, dual_now)
    fitted = project(poly_coef)
    for iteration in range(ITERS):
        early_sum = poly_coef if iteration == 0 else consensus_of(current, dual_now)
        gradient = state_gradient(current)
        descent = gradient + dual_now + rho_local * (current - fitted)
        all_descent = lax.all_gather(descent, "freq", axis=0, tiled=True)
        squares = jnp.sum(all_descent * all_descent, axis=(1, 2))
        totals = lax.psum(squares, "tm")
        scales = jnp.sqrt(totals / (8.0 * K * S) + epsilon)
        own_scale = lax.dynamic_index_in_dim(scales, freq_index, 0, keepdims=False)
        current = current - step_size * descent / own_scale
        poly_coef = early_sum - step_size * jnp.einsum(
            "fj,fcn->jcn", poly_table, all_descent / scales[:, None, None], precision=highest
        )
        fitted = project(poly_coef)
        dual_now = dual_now + rho_local * (current - fitted)
    return (current, dual_now, poly_coef)


def solution(mesh):
    return jax.shard_map(
        body,
        mesh=mesh,
        in_specs=(
            P("tm", "freq", None, None),
            P("tm", "freq", None, None, None),
            P("tm", None, None),
            P("freq", None, "tm"),
            P("freq", None, "tm"),
            P(),
            P(),
        ),
        out_specs=(P("freq", None, "tm"), P("freq", None, "tm"), P(None, None, "tm")),
        check_vma=False,
    )
```

profile of v0, /device:TPU:0, one launch (start us, length us, event | category | flops | bytes accessed | tf_op | source)
XLA Modules:
  0.0 550.6 jit_solution(2707300693803115846)
XLA Ops:
  8.8 0.8 select_reduce_fusion
  9.7 1.5 add_multiply_fusion.1
  11.3 0.8 fusion.14
  12.1 1.2 convert_element_type.5
  13.3 0.8 copy.51
  14.2 37.5 %all-gather.3.cloned.1.call-done = f32[1,8,32768]{2,1,0:T(8,128)} async-done(((f32[1,8,2048]{2,1,0:T(8,128)}), f32[1,8,32768]{2,1,0:T(8,128)}) %all-gather.3.cloned.1.call-update) | async-done | bytes 1048592 | tf_op jit(solution)/shard_map/all_gather | solution.py:129
  51.7 2.9 copy.86
  54.5 2.0 copy.49
  56.6 2.7 gather_fusion
  59.3 3.2 copy.53
  62.5 2.7 gather_fusion.1
  65.2 3.3 copy.50
  68.6 1.1 copy-done.2
  69.9 0.9 add_dynamic-update-slice_fusion.15
  73.0 0.9 add_dynamic-update-slice_fusion.11
  75.3 0.8 add_dynamic-update-slice_fusion.8
  76.1 1.3 reduce_sum.43
  77.4 0.8 copy.70
  78.3 1.0 fusion
  79.2 1.4 negate_reduce_fusion.7
  81.9 1.9 copy.56
  83.9 2.0 copy.55
  86.0 35.9 %scatter_fusion.1 = f32[8,64,512]{1,0,2:T(8,128)S(1)} fusion(f32[8,64,512]{1,0,2:T(8,128)S(1)} %broadcast_in_dim.128.clone.1, s32[512]{0:T(512)S(1)} %compare_select_fusion, f32[512,8,64]{2,1,0:T(8,128)} %copy.56), kind=kCustom, calls=%fused_computation.5 | custom fusion | flops 262144 | bytes 3147776 | tf_op jit(solution)/shard_map/transpose(jvp(jit(_take)))/scatter-add | solution.py:95
  121.9 1.4 broadcast_in_dim.128.clone
  123.3 54.8 %scatter_fusion = f32[8,64,512]{1,0,2:T(8,128)} fusion(f32[8,64,512]{1,0,2:T(8,128)} %broadcast_in_dim.128.clone, s32[512]{0:T(512)S(1)} %compare_select_fusion.1, f32[512,8,64]{2,1,0:T(8,128)} %copy.55), kind=kCustom, calls=%fused_computation.4 | custom fusion | flops 262144 | bytes 3147776 | tf_op jit(solution)/shard_map/transpose(jvp(jit(_take)))/scatter-add | solution.py:96
  178.2 3.2 add_any.896
  181.3 2.2 copy.57
  183.5 1.2 reshape.137
  184.8 56.4 %reduce-scatter.3.cloned.1.call-done = f32[1,8,2048]{2,1,0:T(8,128)} async-done(((f32[1,8,32768]{2,1,0:T(8,128)}), f32[1,8,2048]{2,1,0:T(8,128)}) %reduce-scatter.3.cloned.1.call-update) | async-done | bytes 65552 | tf_op jit(solution)/shard_map/reduce_scatter | solution.py:138
  241.2 0.9 multiply_add_fusion.49
  242.1 4.9 all_gather.13
  247.1 29.7 %psum.29 = f32[2]{0:T(128)S(1)} all-reduce(f32[2]{0:T(128)S(1)} %multiply_reduce_fusion.1), channel_id=1, replica_groups=mesh['tm'=16,'freq'=2] {'tm'}, use_global_device_ids=true, to_apply=%region_7.9 | all-reduce | flops 2 | bytes 16 | tf_op jit(solution)/shard_map/psum | solution.py:152
  278.2 2.2 add_multiply_fusion
  280.4 35.3 %all-gather.5.cloned.1.call-done = f32[1,8,32768]{2,1,0:T(8,128)} async-done(((f32[1,8,2048]{2,1,0:T(8,128)}), f32[1,8,32768]{2,1,0:T(8,128)}) %all-gather.5.cloned.1.call-update) | async-done | bytes 1048592 | tf_op jit(solution)/shard_map/all_gather | solution.py:129
  315.7 2.9 copy.85
  318.6 2.0 copy.58
  320.6 2.8 gather_fusion.3
  323.4 2.9 gather_fusion.2
  326.3 3.3 copy.59
  329.6 2.3 select_bitcast_fusion
  331.9 1.7 copy.61
  333.6 1.5 select_bitcast_fusion.1
  335.2 0.9 add_dynamic-update-slice_fusion.7
  338.3 0.9 add_dynamic-update-slice_fusion.3
  341.4 1.9 reduce_sum.49
  343.3 1.5 copy.71
  344.9 1.0 fusion.1
  345.9 1.4 negate_reduce_fusion.3
  347.7 0.9 multiply_add_fusion.23
  348.6 0.9 multiply_add_fusion.21
  350.0 0.8 copy.64
  350.9 1.3 add_bitcast_fusion.1
  352.2 2.0 copy.63
  354.2 1.4 broadcast_in_dim.128.clone.3
  355.6 49.9 %scatter_fusion.3 = f32[8,64,512]{1,0,2:T(8,128)} fusion(f32[8,64,512]{1,0,2:T(8,128)} %broadcast_in_dim.128.clone.3, s32[512]{0:T(512)S(1)} %compare_select_fusion, f32[512,8,64]{2,1,0:T(8,128)S(1)} %copy.64), kind=kCustom, calls=%fused_computation.7 | custom fusion | flops 262144 | bytes 3147776 | tf_op jit(solution)/shard_map/transpose(jvp(jit(_take)))/scatter-add | solution.py:95
  405.6 35.9 %scatter_fusion.2 = f32[8,64,512]{1,0,2:T(8,128)S(1)} fusion(f32[8,64,512]{1,0,2:T(8,128)S(1)} %broadcast_in_dim.128.clone.2, s32[512]{0:T(512)S(1)} %compare_select_fusion.1, f32[512,8,64]{2,1,0:T(8,128)} %copy.63), kind=kCustom, calls=%fused_computation.6 | custom fusion | flops 262144 | bytes 3147776 | tf_op jit(solution)/shard_map/transpose(jvp(jit(_take)))/scatter-add | solution.py:96
  441.5 3.2 add_any.983
  444.7 2.2 copy.65
  446.9 1.2 reshape.139
  448.1 56.5 %reduce-scatter.5.cloned.1.call-done = f32[1,8,2048]{2,1,0:T(8,128)} async-done(((f32[1,8,32768]{2,1,0:T(8,128)}), f32[1,8,2048]{2,1,0:T(8,128)}) %reduce-scatter.5.cloned.1.call-update) | async-done | bytes 65552 | tf_op jit(solution)/shard_map/reduce_scatter | solution.py:138
  504.6 0.9 add_add_fusion.8
  505.4 4.9 all_gather.15
  510.5 29.5 %psum.30 = f32[2]{0:T(128)S(1)} all-reduce(f32[2]{0:T(128)S(1)} %multiply_reduce_fusion), channel_id=1, replica_groups=mesh['tm'=16,'freq'=2] {'tm'}, use_global_device_ids=true, to_apply=%region_13.15 | all-reduce | flops 2 | bytes 16 | tf_op jit(solution)/shard_map/psum | solution.py:152
  541.4 2.1 multiply_add_fusion.48
  (85 shorter events, 15.2 us)
Async XLA Ops:
  8.0 43.7 %all-gather.3.cloned.1.call-start = ((), (), s32[]{:S(2)}) async-start(), calls=%async_computation.2 | async-start | bytes 1114112 | tf_op jit(solution)/shard_map/all_gather | solution.py:129
  8.7 176.1 %all-reduce.35.cloned.1.call-start = ((), (), s32[]{:S(2)}) async-start(), calls=%async_computation.4 | async-start | bytes 131072 | tf_op jit(solution)/shard_map/psum | solution.py:123
  11.2 229.9 %reduce-scatter.3.cloned.1.call-start = ((), (), s32[]{:S(2)}) async-start(), calls=%async_computation.3 | async-start | bytes 1114112 | tf_op jit(solution)/shard_map/reduce_scatter | solution.py:138
  12.1 56.4 %copy-start.11 = (pred[512]{0:T(512)(128)(4,1)}, pred[512]{0:T(512)(128)(4,1)S(1)}, u32[]{:S(2)}) copy-start(pred[512]{0:T(512)(128)(4,1)S(1)} %compare_and_fusion.1) | copy-start | bytes 1540
  12.1 56.5 %copy-start.12 = (pred[512]{0:T(512)(128)(4,1)}, pred[512]{0:T(512)(128)(4,1)S(1)}, u32[]{:S(2)}) copy-start(pred[512]{0:T(512)(128)(4,1)S(1)} %compare_and_fusion) | copy-start | bytes 1540
  14.2 42.4 %copy-start.9 = (s32[1024]{0:T(1024)}, s32[1024]{0:T(1024)S(1)}, u32[]{:S(2)}) copy-start(s32[1024]{0:T(1024)S(1)} %get-tuple-element.128) | copy-start | bytes 12292
  14.2 48.3 %copy-start.10 = (s32[1024]{0:T(1024)}, s32[1024]{0:T(1024)S(1)}, u32[]{:S(2)}) copy-start(s32[1024]{0:T(1024)S(1)} %get-tuple-element.129) | copy-start | bytes 12292
  65.2 3.3 copy-start.1
  68.5 1.2 copy-start.2
  183.5 57.7 %copy-start.4 = (f32[1,8,2048]{2,1,0:T(8,128)S(1)}, f32[1,8,2048]{2,1,0:T(8,128)}, u32[]{:S(2)}) copy-start(f32[1,8,2048]{2,1,0:T(8,128)} %param.13) | copy-start | bytes 196612
  183.5 57.7 %copy-start.6 = (f32[1,8,2048]{2,1,0:T(8,128)S(1)}, f32[1,8,2048]{2,1,0:T(8,128)}, u32[]{:S(2)}) copy-start(f32[1,8,2048]{2,1,0:T(8,128)} %param.14) | copy-start | bytes 196612
  184.7 131.0 %all-gather.5.cloned.1.call-start = ((), (), s32[]{:S(2)}) async-start(), calls=%async_computation.5 | async-start | bytes 1114112 | tf_op jit(solution)/shard_map/all_gather | solution.py:129
  280.4 224.2 %reduce-scatter.5.cloned.1.call-start = ((), (), s32[]{:S(2)}) async-start(), calls=%async_computation.6 | async-start | bytes 1114112 | tf_op jit(solution)/shard_map/reduce_scatter | solution.py:138
  326.3 5.6 %copy-start = (f32[512,8,64]{2,1,0:T(8,128)S(1)}, f32[512,8,64]{2,1,0:T(8,128)}, u32[]{:S(2)}) copy-start(f32[512,8,64]{2,1,0:T(8,128)} %gather_fusion.2) | copy-start | bytes 3145732
  333.6 1.5 copy-start.3
  349.9 0.9 copy-start.7
  350.0 1.0 copy-start.8
  446.9 94.5 %copy-start.5 = (f32[1,8,2048]{2,1,0:T(8,128)S(1)}, f32[1,8,2048]{2,1,0:T(8,128)}, u32[]{:S(2)}) copy-start(f32[1,8,2048]{2,1,0:T(8,128)} %get-tuple-element.49) | copy-start | bytes 196612
  448.1 93.3 %all-reduce.37.cloned.1.call-start = ((), (), s32[]{:S(2)}) async-start(), calls=%async_computation.7 | async-start | bytes 131072 | tf_op jit(solution)/shard_map/psum | solution.py:123
Sparse Core Ops, SparseCore 0:
  11.0 40.6 all-gather.2
  184.8 56.2 reduce-scatter.2
  280.5 35.1 all-gather.4
  448.2 56.3 reduce-scatter.4
Sparse Core Ops, SparseCore 1:
  12.0 23.2 all-reduce.34
  510.6 19.6 all-reduce.36
where the time goes:
time: 557 us; the launch traced here: 551 us
  other arithmetic  222 us (40%)
  waiting for transfers between devices  186 us (33%)
  blocking collectives  69 us (12%)
  local copies, waits for them, and re-layouts  55.7 us (10%)
  between operations  15.6 us (3%)
    reduce_scatter x2, waiting for transfers between devices, state_gradient(): lax.psum_scatter(grad_term.reshape(1, 8, K * S), 'tm', scatter_dimension=...  113 us
    scatter-add x2, other arithmetic, model_sum(): second_gain = jnp.take(gain_block, second_station, axis=2)  90.7 us
    scatter-add x2, other arithmetic, model_sum(): first_gain = jnp.take(gain_block, first_station, axis=2)  85.8 us
    all_gather x2, waiting for transfers between devices, state_gradient(): gathered = lax.all_gather(current, 'tm', axis=2, tiled=True)  72.8 us
    psum x2, blocking collectives, body(): totals = lax.psum(squares, 'tm')  59.1 us
    gather x4, local copies, waits for them, and re-layouts, model_sum(): first_gain = jnp.take(gain_block, first_station, axis=2)  12.1 us
  transfers between devices with their start and end apart: 6, of which 4 were waited for; matrix products, arithmetic and copies ran while one was open for 25% of the time, Pallas kernels for 0%

commit v1 on v0

v1 whole, which is shorter than its diff:
```python
import functools
import math

import jax
import jax.numpy as jnp
import numpy as np
from jax import lax
from jax.experimental import pallas as pl
from jax.experimental.pallas import tpu as pltpu
from jax.sharding import PartitionSpec as P

ITERS = 2
MESH = pl.DeviceIdType.MESH
ROWS = 8

step_size = 0.5
epsilon = 1e-06


def poly_basis(channels, degrees):
    points = np.linspace(-1.0, 1.0, channels)
    columns = []
    for degree in range(degrees):
        column = points**degree
        for earlier in columns:
            column = column - np.dot(earlier, column) * earlier
        column = column / np.sqrt(np.dot(column, column))
        columns.append(column)
    return np.stack(columns, axis=1).astype(np.float32)


def split_entries(parts):
    return [[(parts[4 * i + 2 * j], parts[4 * i + 2 * j + 1]) for j in range(2)] for i in range(2)]


def join_entries(mat):
    return [part for row in mat for entry in row for part in entry]


def times_pair(a, b):
    return (a[0] * b[0] - a[1] * b[1], a[0] * b[1] + a[1] * b[0])


def times_conj(a, b):
    return (a[0] * b[0] + a[1] * b[1], a[1] * b[0] - a[0] * b[1])


def add_pairs(a, b):
    return (a[0] + b[0], a[1] + b[1])


def mat_mul(a, b):
    return [[add_pairs(times_pair(a[i][0], b[0][j]), times_pair(a[i][1], b[1][j])) for j in range(2)] for i in range(2)]


def mat_mul_right_h(a, b):
    return [[add_pairs(times_conj(a[i][0], b[j][0]), times_conj(a[i][1], b[j][1])) for j in range(2)] for i in range(2)]


def mat_mul_left_h(a, b):
    return [[add_pairs(times_conj(b[0][j], a[0][i]), times_conj(b[1][j], a[1][i])) for j in range(2)] for i in range(2)]


def kernel(
    T, F, nd, S, K, N, basis, weight,
    vis_ref, coh_ref, st_ref, jones_ref, dual_ref, cluster_ref, table_ref,
    jones_out, dual_out, poly_out,
    coh_in, coh32, st_all, oh, tab, gp, abuf, xbuf, partial, part_in, res, acc, jn, du, de, fit, rho, sq,
    st_ss, st_rs, coh_ss, coh_rs, pa_ss, pa_rs, re_ss, re_rs, in_ss, in_rs, de_ss, de_rs, sq_ss, sq_rs,
):
    me = lax.axis_index("tm")
    fi = lax.axis_index("freq")
    g = ROWS // nd
    groups = T // g
    L = nd * S
    degrees = basis.shape[1]
    own_group = me // g

    def st_copy(src, to):
        return pltpu.make_async_remote_copy(
            src_ref=st_all.at[src], dst_ref=st_all.at[src], send_sem=st_ss.at[to], recv_sem=st_rs.at[src],
            device_id={"tm": to}, device_id_type=MESH)

    def coh_copy(src, to):
        return pltpu.make_async_remote_copy(
            src_ref=coh_ref.at[to], dst_ref=coh_in.at[src], send_sem=coh_ss.at[to], recv_sem=coh_rs.at[src],
            device_id={"tm": to}, device_id_type=MESH)

    def part_copy(it, src, to):
        return pltpu.make_async_remote_copy(
            src_ref=partial.at[it, to], dst_ref=part_in.at[it, src], send_sem=pa_ss.at[it, to],
            recv_sem=pa_rs.at[it, src], device_id={"tm": to}, device_id_type=MESH)

    def res_copy(it, src, to):
        return pltpu.make_async_remote_copy(
            src_ref=res.at[it, src], dst_ref=res.at[it, src], send_sem=re_ss.at[it, to],
            recv_sem=re_rs.at[it, src], device_id={"tm": to}, device_id_type=MESH)

    def state_copy(which, src, to):
        ref = (jn, du)[which]
        return pltpu.make_async_remote_copy(
            src_ref=ref.at[src], dst_ref=ref.at[src], send_sem=in_ss.at[which, to], recv_sem=in_rs.at[which, src],
            device_id={"freq": to}, device_id_type=MESH)

    def de_copy(it, src, to):
        return pltpu.make_async_remote_copy(
            src_ref=de.at[it, src], dst_ref=de.at[it, src], send_sem=de_ss.at[it, to], recv_sem=de_rs.at[it, src],
            device_id={"freq": to}, device_id_type=MESH)

    def sq_copy(it, to_f, to_t):
        mine = fi * T + me
        return pltpu.make_async_remote_copy(
            src_ref=sq.at[it, mine], dst_ref=sq.at[it, mine], send_sem=sq_ss.at[it], recv_sem=sq_rs.at[it],
            device_id={"tm": to_t, "freq": to_f}, device_id_type=MESH)

    def sq_all(it):
        span = sq.at[it, pl.ds(0, F * T - 1)]
        return pltpu.make_async_remote_copy(
            src_ref=span, dst_ref=span, send_sem=sq_ss.at[it], recv_sem=sq_rs.at[it],
            device_id={"tm": me, "freq": fi}, device_id_type=MESH)

    def each_peer(fn):
        def one(o, _):
            fn(lax.rem(me + o, T))
            return 0
        lax.fori_loop(1, T, one, 0)

    def each_other(fn):
        def one(o, _):
            fn(lax.rem(fi * T + me + o, F * T))
            return 0
        lax.fori_loop(1, F * T, one, 0)

    st_all[me] = st_ref[...]
    jn[fi] = jones_ref[...]
    du[fi] = dual_ref[...]
    barrier = pltpu.get_barrier_semaphore()

    def greet(d):
        pl.semaphore_signal(barrier, inc=1, device_id={"tm": lax.rem(d, T), "freq": d // T}, device_id_type=MESH)

    each_other(greet)
    pl.semaphore_wait(barrier, F * T - 1)

    each_peer(lambda j: st_copy(me, j).start())
    each_peer(lambda j: coh_copy(me, j).start())
    for o in range(1, F):
        to = lax.rem(fi + o, F)
        state_copy(0, fi, to).start()
        state_copy(1, fi, to).start()
    coh_in[me] = coh_ref[me]

    for d in range(nd):
        value = table_ref[cluster_ref[me * nd + d]]
        rho[:, d * S:(d + 1) * S] = jnp.full((ROWS, S), value, jnp.float32)

    slot_n = lax.broadcasted_iota(jnp.int32, (ROWS, N), 0) // nd
    slot_c = lax.broadcasted_iota(jnp.int32, (ROWS, 128), 0) // nd

    def set_table():
        now = jn[fi]
        for d in range(nd):
            piece = now[:, d * S:(d + 1) * S]
            high = piece.astype(jnp.bfloat16).astype(jnp.float32)
            low = piece - high
            for s in range(g):
                for q in range(S // 128):
                    part = high if s % 2 == 0 else low
                    tab[q, pl.ds(s * nd + d, 8, stride=8), :] = part[:, q * 128:(q + 1) * 128]

    def gather_group(it, p):
        packed = [None, None]
        table = jnp.concatenate([tab[q] for q in range(S // 128)], axis=1).astype(jnp.bfloat16)
        for tt in range(g):
            t = p * g + tt
            if it == 0:
                @pl.when(t != me)
                def _():
                    st_copy(t, me).wait_recv()
                for e in range(2):
                    row = st_all[t, e:e + 1, :]
                    for lo in range(0, S, 64):
                        ids = lax.broadcasted_iota(jnp.int32, (64, N), 0) + lo
                        oh[t, e, lo:lo + 64, :] = jnp.where(ids == row, 1.0, 0.0).astype(jnp.bfloat16)
            for e in range(2):
                got = jnp.dot(table, oh[t, e], preferred_element_type=jnp.float32)
                tiles = []
                for c in range(8):
                    tile = got[8 * c:8 * c + 8, :]
                    tile = tile + pltpu.roll(tile, nd, 0)
                    tiles.append(tile if tt == 0 else jnp.where(slot_n == tt, tile, packed[e][c]))
                packed[e] = tiles
        for e in range(2):
            for c in range(8):
                gp[p, e, c] = packed[e][c]

    def forward_group(it, p):
        if it == 0:
            tiles = []
            for tt in range(g):
                t = p * g + tt

                @pl.when(t != me)
                def _():
                    coh_copy(t, me).wait_recv()
                tiles.append(coh_in[t].astype(jnp.float32))
            for c in range(8):
                out = None
                for tt in range(g):
                    tile = tiles[tt][8 * (c // g):8 * (c // g) + 8, :]
                    shift = ((tt - c % g) % g) * nd
                    if shift:
                        tile = pltpu.roll(tile, shift, 0)
                    out = tile if tt == 0 else jnp.where(slot_n == tt, tile, out)
                coh32[p, c] = out
        for lo in range(0, N, 128):
            lanes = slice(lo, lo + 128)
            first = split_entries([gp[p, 0, c, :, lanes] for c in range(8)])
            second = split_entries([gp[p, 1, c, :, lanes] for c in range(8)])
            sky = split_entries([coh32[p, c, :, lanes] for c in range(8)])
            prod = mat_mul(first, sky)
            for c, part in enumerate(join_entries(prod)):
                abuf[p, c, :, lanes] = part
            model = join_entries(mat_mul_right_h(prod, second))
            for c in range(8):
                total = model[c]
                width = 1
                while width < nd:
                    total = total + pltpu.roll(total, ROWS - width, 0)
                    width *= 2
                for tt in range(g):
                    partial[it, p * g + tt, c:c + 1, lanes] = total[tt * nd:tt * nd + 1, :]
        for tt in range(g):
            t = p * g + tt

            @pl.when(t != me)
            def _():
                part_copy(it, me, t).start()

    def backward_group(it, p):
        for tt in range(g):
            t = p * g + tt

            @pl.when(t != me)
            def _():
                res_copy(it, t, me).wait_recv()
        for lo in range(0, N, 128):
            lanes = slice(lo, lo + 128)
            prod = split_entries([abuf[p, c, :, lanes] for c in range(8)])
            second = split_entries([gp[p, 1, c, :, lanes] for c in range(8)])
            sky = split_entries([coh32[p, c, :, lanes] for c in range(8)])
            resid = []
            for c in range(8):
                out = None
                for tt in range(g):
                    row = jnp.broadcast_to(res[it, p * g + tt, c:c + 1, lanes], (ROWS, 128))
                    out = row if tt == 0 else jnp.where(slot_c == tt, row, out)
                resid.append(out)
            resid = split_entries(resid)
            grads = (
                join_entries(mat_mul(resid, mat_mul_right_h(second, sky))),
                join_entries(mat_mul_left_h(resid, prod)),
            )
            for e in range(2):
                highs = [x.astype(jnp.bfloat16).astype(jnp.float32) for x in grads[e]]
                lows = [pltpu.roll(x - h, nd, 0) for x, h in zip(grads[e], highs)]
                for tt in range(g):
                    outs = []
                    for h, l in zip(highs, lows):
                        rest = l if g == 2 else jnp.where(slot_c == (tt + 1) % g, l, 0.0)
                        outs.append(jnp.where(slot_c == tt, h, rest))
                    xbuf[e, tt, :, lanes] = jnp.concatenate(outs, axis=0).astype(jnp.bfloat16)
        total = jnp.concatenate([acc[q] for q in range(S // 128)], axis=1)
        for tt in range(g):
            for e in range(2):
                total = total + lax.dot_general(
                    xbuf[e, tt], oh[p * g + tt, e], (((1,), (1,)), ((), ())), preferred_element_type=jnp.float32)
        for q in range(S // 128):
            acc[q] = total[:, q * 128:(q + 1) * 128]

    def consensus():
        sums = [jn[f] + du[f] / rho[...] for f in range(F)]
        for j in range(degrees):
            total = None
            for f in range(F):
                term = float(basis[f, j]) * sums[f]
                total = term if total is None else total + term
            poly_out[j] = total
        for f in range(F):
            total = None
            for j in range(degrees):
                term = float(basis[f, j]) * poly_out[j]
                total = term if total is None else total + term
            fit[f] = total

    set_table()

    for it in range(ITERS):
        def gather_step(i, _):
            gather_group(it, lax.rem(own_group - 1 - i + 2 * groups, groups))
            return 0

        def forward_step(i, _):
            forward_group(it, lax.rem(own_group - 1 - i + 2 * groups, groups))
            return 0

        def backward_step(i, _):
            backward_group(it, lax.rem(own_group - 1 - i + 2 * groups, groups))
            return 0

        lax.fori_loop(0, groups, gather_step, 0)
        lax.fori_loop(0, groups, forward_step, 0)
        if it == 0:
            for o in range(1, F):
                other = lax.rem(fi + o, F)
                state_copy(0, other, fi).wait_recv()
                state_copy(1, other, fi).wait_recv()
            consensus()

        def add_part(o, total):
            src = lax.rem(me - o + T, T)
            part_copy(it, src, me).wait_recv()
            return total + part_in[it, src]

        model = lax.fori_loop(1, T, add_part, partial[it, me])
        res[it, me] = weight * (model - vis_ref[...])
        each_peer(lambda j: res_copy(it, me, j).start())
        acc[...] = jnp.zeros_like(acc)
        lax.fori_loop(0, groups, backward_step, 0)

        for d in range(nd):
            for q in range(S // 128):
                total = None
                for s in range(g):
                    term = acc[q, pl.ds(s * nd + d, 8, stride=8), :]
                    total = term if total is None else total + term
                de[it, fi, :, d * S + q * 128:d * S + (q + 1) * 128] = total
        descent = de[it, fi] + du[fi] + rho[...] * (jn[fi] - fit[fi])
        de[it, fi] = descent
        squares = descent * descent
        total = squares[:, 0:128]
        for lo in range(128, L, 128):
            total = total + squares[:, lo:lo + 128]
        sq[it, fi * T + me] = total
        each_other(lambda d: sq_copy(it, d // T, lax.rem(d, T)).start())
        for o in range(1, F):
            de_copy(it, fi, lax.rem(fi + o, F)).start()
        sq_all(it).wait_recv()
        for o in range(1, F):
            de_copy(it, lax.rem(fi + o, F), fi).wait_recv()
        if it == 0:
            for o in range(1, F):
                other = lax.rem(fi + o, F)
                state_copy(0, fi, other).wait_send()
                state_copy(1, fi, other).wait_send()
        for f in range(F):
            tile = jnp.sum(sq[it, pl.ds(f * T, T)], axis=0)
            whole = jnp.sum(jnp.sum(tile, axis=1, keepdims=True), axis=0, keepdims=True)
            scale = jnp.sqrt(whole / (8.0 * K * S) + epsilon)
            jn[f] = jn[f] - step_size * de[it, f] / scale
        if it + 1 < ITERS:
            set_table()
        consensus()
        for f in range(F):
            du[f] = du[f] + rho[...] * (jn[f] - fit[f])

    jones_out[...] = jn[fi]
    dual_out[...] = du[fi]

    def drain(j):
        st_copy(me, j).wait_send()
        coh_copy(me, j).wait_send()
        for it in range(ITERS):
            part_copy(it, me, j).wait_send()
            res_copy(it, me, j).wait_send()

    each_peer(drain)
    for it in range(ITERS):
        sq_all(it).wait_send()
        for o in range(1, F):
            de_copy(it, fi, lax.rem(fi + o, F)).wait_send()


def body(visibilities, coherency, stations, jones, dual, cluster, rho_table):
    T = lax.axis_size("tm")
    F = lax.axis_size("freq")
    K, N = coherency.shape[3], coherency.shape[4]
    L = jones.shape[2]
    nd = K // T
    S = L // nd
    g = ROWS // nd
    basis = poly_basis(F, min(3, F - 1))
    degrees = basis.shape[1]
    weight = np.float32(math.sqrt(S / (2.0 * T * N)))
    blocks = coherency[0, 0].reshape(8, T, nd, N).transpose(1, 0, 2, 3).reshape(T, 8 * nd, N)
    vmem = pl.BlockSpec(memory_space=pltpu.VMEM)
    smem = pl.BlockSpec(memory_space=pltpu.SMEM)
    f32, bf16 = jnp.float32, jnp.bfloat16
    dma = pltpu.SemaphoreType.DMA
    jones_out, dual_out, poly = pl.pallas_call(
        functools.partial(kernel, T, F, nd, S, K, N, basis, weight),
        out_shape=(
            jax.ShapeDtypeStruct((8, L), f32),
            jax.ShapeDtypeStruct((8, L), f32),
            jax.ShapeDtypeStruct((degrees, 8, L), f32),
        ),
        in_specs=[vmem] * 5 + [smem] * 2,
        out_specs=(vmem, vmem, vmem),
        scratch_shapes=[
            pltpu.VMEM((T, 8 * nd, N), bf16),
            pltpu.VMEM((T // g, 8, 8, N), f32),
            pltpu.VMEM((T, 2, N), jnp.int32),
            pltpu.VMEM((T, 2, S, N), bf16),
            pltpu.VMEM((S // 128, 64, 128), f32),
            pltpu.VMEM((T // g, 2, 8, 8, N), f32),
            pltpu.VMEM((T // g, 8, 8, N), f32),
            pltpu.VMEM((2, g, 64, N), bf16),
            pltpu.VMEM((ITERS, T, 8, N), f32),
            pltpu.VMEM((ITERS, T, 8, N), f32),
            pltpu.VMEM((ITERS, T, 8, N), f32),
            pltpu.VMEM((S // 128, 64, 128), f32),
            pltpu.VMEM((F, 8, L), f32),
            pltpu.VMEM((F, 8, L), f32),
            pltpu.VMEM((ITERS, F, 8, L), f32),
            pltpu.VMEM((F, 8, L), f32),
            pltpu.VMEM((8, L), f32),
            pltpu.VMEM((ITERS, F * T, 8, 128), f32),
            dma((T,)), dma((T,)), dma((T,)), dma((T,)),
            dma((ITERS, T)), dma((ITERS, T)), dma((ITERS, T)), dma((ITERS, T)),
            dma((2, F)), dma((2, F)), dma((ITERS, F)), dma((ITERS, F)), dma((ITERS,)), dma((ITERS,)),
        ],
        compiler_params=pltpu.CompilerParams(
            collective_id=0, has_side_effects=True, vmem_limit_bytes=56 * 1024 * 1024),
        cost_estimate=pl.CostEstimate(flops=10**10, bytes_accessed=10**7, transcendentals=0),
    )(visibilities[0, 0], blocks, stations[0], jones[0], dual[0], cluster, rho_table)
    return jones_out[None], dual_out[None], poly


def solution(mesh):
    return jax.shard_map(
        body,
        mesh=mesh,
        in_specs=(
            P("tm", "freq", None, None),
            P("tm", "freq", None, None, None),
            P("tm", None, None),
            P("freq", None, "tm"),
            P("freq", None, "tm"),
            P(),
            P(),
        ),
        out_specs=(P("freq", None, "tm"), P("freq", None, "tm"), P(None, None, "tm")),
        check_vma=False,
    )
```

time: 557 us -> 83.2 us (0.15); the launches traced: 551 us -> 82.9 us
  other arithmetic: 222 us -> 0 us
  waiting for transfers between devices: 186 us -> 0 us
  Pallas kernels: 0 us -> 76.9 us
  blocking collectives: 69 us -> 0 us
  local copies, waits for them, and re-layouts: 55.7 us -> 5.32 us
  between operations: 15.6 us -> 0.66 us
    scatter-add x4 -> x0, other arithmetic: 177 us -> none  [the longest x2 90.7 us: model_sum(): second_gain = jnp.take(gain_block, second_station, axis=2)]
    reduce_scatter x2 -> x0, waiting for transfers between devices: 113 us -> none  [state_gradient(): lax.psum_scatter(grad_term.reshape(1, 8, K * S), 'tm', scatter_dimension=...]
    pallas_call x0 -> x1, Pallas kernels: none -> 76.9 us  [body(): pl.pallas_call(functools.partial(kernel, T, F, nd, S, K, N, basis, weight...]
    all_gather x2 -> x0, waiting for transfers between devices: 72.8 us -> none  [state_gradient(): gathered = lax.all_gather(current, 'tm', axis=2, tiled=True)]
    psum x2 -> x0, blocking collectives: 59.1 us -> none  [body(): totals = lax.psum(squares, 'tm')]
    gather x8 -> x0, local copies, waits for them, and re-layouts: 22.6 us -> none  [the longest x4 12.1 us: model_sum(): first_gain = jnp.take(gain_block, first_station, axis=2)]
    add_any x18 -> x0, other arithmetic: 11.4 us -> none  [the longest x2 6.31 us: model_sum(): first_gain = jnp.take(gain_block, first_station, axis=2)]
    add_any x6 -> x0, local copies, waits for them, and re-layouts: 11 us -> none  [the longest x4 6.67 us: split_entries(): stacked[4 * left_index + 2 * right_index]]
  transfers between devices with their start and end apart: 6 -> 0, of which waited for: 4 -> 0; matrix products, arithmetic and copies ran while one was open for 25% -> 0% of each run, Pallas kernels for 0% -> 0%
where the time goes in v1:
time: 83.2 us; the launch traced here: 82.9 us
  Pallas kernels  76.9 us (92%)
  local copies, waits for them, and re-layouts  5.32 us (6%)
    pallas_call x1, Pallas kernels, body(): pl.pallas_call(functools.partial(kernel, T, F, nd, S, K, N, basis, weight...  76.9 us
    unnamed x7, local copies, waits for them, and re-layouts  3 us

profile of v1, /device:TPU:0, one launch (start us, length us, event | category | flops | bytes accessed | tf_op | source)
XLA Modules:
  0.0 82.9 jit_solution(17501264977372655780)
XLA Ops:
  0.6 1.2 %reshape_squeeze.3 = bf16[8,16,4,512]{3,2,1,0:T(4,128)(2,1)S(1)} reshape(bf16[1,1,8,64,512]{4,3,2,1,0:T(8,128)(2,1)} %param.8) | data formatting | bytes 1048576 | tf_op jit(solution)/shard_map/reshape;squeeze | solution.py:395
  1.8 0.2 copy.12
  2.0 0.9 %reshape.9.coh_ref = bf16[16,32,512]{2,1,0:T(8,128)(2,1)} reshape(bf16[16,8,4,512]{3,2,1,0:T(4,128)(2,1)S(1)} %bitcast.11) | data formatting | bytes 1048576 | tf_op jit(solution)/shard_map/reshape | solution.py:395
  3.0 76.9 %shard_map.94 = (f32[8,2048]{1,0:T(8,128)}, f32[8,2048]{1,0:T(8,128)}, f32[1,8,2048]{2,1,0:T(8,128)}) custom-call(f32[8,512]{1,0:T(8,128)} %bitcast.16, bf16[16,32,512]{2,1,0:T(8,128)(2,1)} %reshape.9.coh_ref, s32[2,512]{1,0:T(2,128)} %bitcast.17, f32[8,2048]{1,0:T(8,128)} %bitcast.14, f32[8,2048]{1,0:T(8,128)} %bitcast.15, s32[64]{0:T(128)} %cluster_ref.1, ...), custom_call_target="tpu_custom_call" | custom-call | flops 10000000000 | bytes 10000000 | tf_op jit(solution)/shard_map/pallas_call | solution.py:400
  79.9 0.0 copy-start.1
  79.9 1.5 %copy.16 = f32[1,8,2048]{2,1,0:T(8,128)} copy(f32[1,8,2048]{2,1,0:T(8,128)} %bitcast.13) | data formatting | bytes 131072
  81.4 0.0 copy-done.1
  81.4 0.0 copy-start
  81.4 0.6 copy.17
  82.1 0.2 copy-done
  82.3 0.6 copy.18
Async XLA Ops:
  79.9 1.5 %copy-start.1 = (f32[8,2048]{1,0:T(8,128)S(1)}, f32[8,2048]{1,0:T(8,128)}, u32[]{:S(2)}) copy-start(f32[8,2048]{1,0:T(8,128)} %get-tuple-element.7) | copy-start | bytes 196612
  81.4 0.9 %copy-start = (f32[1,8,2048]{2,1,0:T(8,128)S(1)}, f32[1,8,2048]{2,1,0:T(8,128)}, u32[]{:S(2)}) copy-start(f32[1,8,2048]{2,1,0:T(8,128)} %get-tuple-element.14) | copy-start | bytes 196612

commit v2 on v1

v2 whole, which is shorter than its diff:
```python
import functools
import math

import jax
import jax.numpy as jnp
import numpy as np
from jax import lax
from jax.experimental import pallas as pl
from jax.experimental.pallas import tpu as pltpu
from jax.sharding import PartitionSpec as P

ITERS = 2
MESH = pl.DeviceIdType.MESH
ROWS = 8

step_size = 0.5
epsilon = 1e-06


def poly_basis(channels, degrees):
    points = np.linspace(-1.0, 1.0, channels)
    columns = []
    for degree in range(degrees):
        column = points**degree
        for earlier in columns:
            column = column - np.dot(earlier, column) * earlier
        column = column / np.sqrt(np.dot(column, column))
        columns.append(column)
    return np.stack(columns, axis=1).astype(np.float32)


def split_entries(parts):
    return [[(parts[4 * i + 2 * j], parts[4 * i + 2 * j + 1]) for j in range(2)] for i in range(2)]


def join_entries(mat):
    return [part for row in mat for entry in row for part in entry]


def times_pair(a, b):
    return (a[0] * b[0] - a[1] * b[1], a[0] * b[1] + a[1] * b[0])


def times_conj(a, b):
    return (a[0] * b[0] + a[1] * b[1], a[1] * b[0] - a[0] * b[1])


def add_pairs(a, b):
    return (a[0] + b[0], a[1] + b[1])


def mat_mul(a, b):
    return [[add_pairs(times_pair(a[i][0], b[0][j]), times_pair(a[i][1], b[1][j])) for j in range(2)] for i in range(2)]


def mat_mul_right_h(a, b):
    return [[add_pairs(times_conj(a[i][0], b[j][0]), times_conj(a[i][1], b[j][1])) for j in range(2)] for i in range(2)]


def mat_mul_left_h(a, b):
    return [[add_pairs(times_conj(b[0][j], a[0][i]), times_conj(b[1][j], a[1][i])) for j in range(2)] for i in range(2)]


def kernel(
    T, F, Z, nd, S, K, N, basis, weight,
    vis_ref, coh_hbm, st_ref, jones_ref, dual_ref, cluster_ref, table_ref,
    jones_out, dual_out, poly_out,
    coh_raw, coh_out, coh_in, st_all, oh, tab, tabs, gz, zde, gp, abuf, xbuf, partial, part_in, res, acc, gout, gin,
    jn, du, de, fit, rho, sq,
    raw_sem, st_ss, st_rs, coh_ss, coh_rs, gz_ss, gz_rs, zd_ss, zd_rs, pa_ss, pa_rs, re_ss, re_rs, go_ss, go_rs,
    in_ss, in_rs, de_ss, de_rs, sq_ss, sq_rs,
):
    me = lax.axis_index("tm")
    fi = lax.axis_index("freq")
    Q = T // Z
    z, q = me // Q, lax.rem(me, Q)
    D = Z * nd
    tiles = D // ROWS
    g = ROWS // nd
    L = nd * S
    lane_tiles = S // 128
    degrees = basis.shape[1]

    def remote(src, dst, send, recv, to):
        return pltpu.make_async_remote_copy(
            src_ref=src, dst_ref=dst, send_sem=send, recv_sem=recv, device_id=to, device_id_type=MESH)

    def plane(u):
        return {"tm": z * Q + u}

    def column(v):
        return {"tm": v * Q + q}

    def st_copy(src, to):
        return remote(st_all.at[src], st_all.at[src], st_ss.at[to], st_rs.at[src], plane(to))

    def coh_copy(src, to):
        return remote(coh_out.at[to], coh_in.at[src], coh_ss.at[to], coh_rs.at[src], plane(to))

    def part_copy(it, src, to):
        return remote(partial.at[it, to], part_in.at[it, src], pa_ss.at[it, to], pa_rs.at[it, src], plane(to))

    def res_copy(it, src, to):
        return remote(res.at[it, src], res.at[it, src], re_ss.at[it, to], re_rs.at[it, src], plane(to))

    def gz_copy(src, to):
        return remote(gz.at[src], gz.at[src], gz_ss.at[to], gz_rs.at[src], column(to))

    def zd_copy(it, src, to):
        return remote(de.at[it, fi], zde.at[it, src], zd_ss.at[it, to], zd_rs.at[it, src], column(to))

    def go_copy(it, src, to):
        return remote(gout.at[it, to], gin.at[it, src], go_ss.at[it, to], go_rs.at[it, src], column(to))

    def state_copy(which, src, to):
        ref = (jn, du)[which]
        return remote(ref.at[src], ref.at[src], in_ss.at[which, to], in_rs.at[which, src], {"freq": to})

    def de_copy(it, src, to):
        return remote(de.at[it, src], de.at[it, src], de_ss.at[it, to], de_rs.at[it, src], {"freq": to})

    def sq_copy(it, to_f, to_t):
        mine = fi * T + me
        return remote(sq.at[it, mine], sq.at[it, mine], sq_ss.at[it], sq_rs.at[it], {"tm": to_t, "freq": to_f})

    def sq_all(it):
        span = sq.at[it, pl.ds(0, F * T - 1)]
        return remote(span, span, sq_ss.at[it], sq_rs.at[it], {"tm": me, "freq": fi})

    def each_other(fn):
        def one(o, _):
            fn(lax.rem(fi * T + me + o, F * T))
            return 0
        lax.fori_loop(1, F * T, one, 0)

    plane_next = [lax.rem(q + o, Q) for o in range(1, Q)]
    plane_from = [lax.rem(q - o + Q, Q) for o in range(1, Q)]
    column_others = [lax.rem(z + o, Z) for o in range(1, Z)]
    freq_others = [lax.rem(fi + o, F) for o in range(1, F)]

    raw = pltpu.make_async_copy(coh_hbm, coh_raw, raw_sem)
    raw.start()
    barrier = pltpu.get_barrier_semaphore()

    def greet(d):
        pl.semaphore_signal(barrier, inc=1, device_id={"tm": lax.rem(d, T), "freq": d // T}, device_id_type=MESH)

    each_other(greet)
    st_all[q] = st_ref[...]
    gz[z] = jones_ref[...]
    jn[fi] = jones_ref[...]
    du[fi] = dual_ref[...]
    for d in range(nd):
        value = table_ref[cluster_ref[me * nd + d]]
        rho[:, d * S:(d + 1) * S] = jnp.full((ROWS, S), value, jnp.float32)
    pl.semaphore_wait(barrier, F * T - 1)

    for to in plane_next:
        st_copy(q, to).start()
    for to in column_others:
        gz_copy(z, to).start()
    raw.wait()

    slot = lax.broadcasted_iota(jnp.int32, (ROWS, N), 0) // nd
    for c in range(8):
        full = coh_raw[c].astype(jnp.float32)
        for u in range(Q):
            rows = []
            for m in range(tiles):
                out = None
                for s in range(g):
                    unit = (m * g + s) * Q + u
                    tile = full[8 * (unit // g):8 * (unit // g) + 8, :]
                    shift = ((s - unit % g) % g) * nd
                    if shift:
                        tile = pltpu.roll(tile, shift, 0)
                    out = tile if s == 0 else jnp.where(slot == s, tile, out)
                rows.append(out)
            block = rows[0] if tiles == 1 else jnp.concatenate(rows, axis=0)
            coh_out[u, c * D:(c + 1) * D, :] = block.astype(jnp.bfloat16)
    for to in plane_next:
        coh_copy(q, to).start()
    coh_in[q] = coh_out[q]
    for to in freq_others:
        state_copy(0, fi, to).start()
        state_copy(1, fi, to).start()

    def build(i, _):
        u = lax.rem(q - i + Q, Q)

        @pl.when(u != q)
        def _():
            st_copy(u, q).wait_recv()
        for e in range(2):
            row = st_all[u, e:e + 1, :]
            for lo in range(0, S, 64):
                ids = lax.broadcasted_iota(jnp.int32, (64, N), 0) + lo
                oh[u, e, lo:lo + 64, :] = jnp.where(ids == row, 1.0, 0.0).astype(jnp.bfloat16)
        return 0

    lax.fori_loop(0, Q, build, 0)

    def set_table():
        for v in range(Z):
            now = gz[v]
            for d in range(nd):
                piece = now[:, d * S:(d + 1) * S]
                high = piece.astype(jnp.bfloat16).astype(jnp.float32)
                low = piece - high
                for k in range(lane_tiles):
                    lanes = slice(k * 128, (k + 1) * 128)
                    tabs[0, k, pl.ds(v * nd + d, 8, stride=D), :] = high[:, lanes]
                    tabs[1, k, pl.ds(v * nd + d, 8, stride=D), :] = low[:, lanes]
        for h in range(2):
            for k in range(lane_tiles):
                tab[h, :, k * 128:(k + 1) * 128] = tabs[h, k].astype(jnp.bfloat16)

    def gather_time(u):
        for e in range(2):
            gp[u, e] = (
                jnp.dot(tab[0], oh[u, e], preferred_element_type=jnp.float32)
                + jnp.dot(tab[1], oh[u, e], preferred_element_type=jnp.float32))

    def tile_rows(c, m):
        return slice(c * D + m * ROWS, c * D + (m + 1) * ROWS)

    def sky_tiles(u, lanes):
        sky = [coh_in[u, c * D:(c + 1) * D, lanes].astype(jnp.float32) for c in range(8)]
        return [split_entries([part[m * ROWS:(m + 1) * ROWS] for part in sky]) for m in range(tiles)]

    def forward_time(it, u):
        for lo in range(0, N, 128):
            lanes = slice(lo, lo + 128)
            sky = sky_tiles(u, lanes)
            sums = None
            for m in range(tiles):
                first = split_entries([gp[u, 0, tile_rows(c, m), lanes] for c in range(8)])
                second = split_entries([gp[u, 1, tile_rows(c, m), lanes] for c in range(8)])
                prod = mat_mul(first, sky[m])
                for c, part in enumerate(join_entries(prod)):
                    abuf[u, tile_rows(c, m), lanes] = part
                model = join_entries(mat_mul_right_h(prod, second))
                sums = model if sums is None else [x + y for x, y in zip(sums, model)]
            for c in range(8):
                partial[it, u, c:c + 1, lanes] = jnp.sum(sums[c], axis=0, keepdims=True)

        @pl.when(u != q)
        def _():
            part_copy(it, q, u).start()

    def backward_time(it, u):
        @pl.when(u != q)
        def _():
            res_copy(it, u, q).wait_recv()
        for lo in range(0, N, 128):
            lanes = slice(lo, lo + 128)
            sky = sky_tiles(u, lanes)
            resid = split_entries([
                jnp.broadcast_to(res[it, u, c:c + 1, lanes], (ROWS, 128)) for c in range(8)])
            grads = [[None] * (8 * tiles), [None] * (8 * tiles)]
            for m in range(tiles):
                prod = split_entries([abuf[u, tile_rows(c, m), lanes] for c in range(8)])
                second = split_entries([gp[u, 1, tile_rows(c, m), lanes] for c in range(8)])
                first_grad = join_entries(mat_mul(resid, mat_mul_right_h(second, sky[m])))
                second_grad = join_entries(mat_mul_left_h(resid, prod))
                for c in range(8):
                    grads[0][c * tiles + m] = first_grad[c]
                    grads[1][c * tiles + m] = second_grad[c]
            for e in range(2):
                for pair in range(4 * tiles):
                    both = jnp.concatenate(grads[e][2 * pair:2 * pair + 2], axis=0)
                    high = both.astype(jnp.bfloat16)
                    low = (both - high.astype(jnp.float32)).astype(jnp.bfloat16)
                    xbuf[0, e, 16 * pair:16 * pair + 16, lanes] = high
                    xbuf[1, e, 16 * pair:16 * pair + 16, lanes] = low
        for k in range(lane_tiles):
            total = acc[k]
            for e in range(2):
                for h in range(2):
                    total = total + lax.dot_general(
                        xbuf[h, e], oh[u, e, k * 128:(k + 1) * 128, :], (((1,), (1,)), ((), ())),
                        preferred_element_type=jnp.float32)
            acc[k] = total

    def consensus():
        sums = [jn[f] + du[f] / rho[...] for f in range(F)]
        for j in range(degrees):
            total = None
            for f in range(F):
                term = float(basis[f, j]) * sums[f]
                total = term if total is None else total + term
            poly_out[j] = total
        for f in range(F):
            total = None
            for j in range(degrees):
                term = float(basis[f, j]) * poly_out[j]
                total = term if total is None else total + term
            fit[f] = total

    for v in column_others:
        gz_copy(v, z).wait_recv()

    for it in range(ITERS):
        set_table()
        if it == 0:
            def gather_step(i, _):
                gather_time(lax.rem(q - i + Q, Q))
                return 0

            def forward_step(i, _):
                u = lax.rem(q - i + Q, Q)

                @pl.when(u != q)
                def _():
                    coh_copy(u, q).wait_recv()
                forward_time(it, u)
                return 0

            lax.fori_loop(0, Q, gather_step, 0)
            lax.fori_loop(0, Q, forward_step, 0)
            for f in freq_others:
                state_copy(0, f, fi).wait_recv()
                state_copy(1, f, fi).wait_recv()
            consensus()
        else:
            def both_step(i, _):
                u = lax.rem(q + 1 + i, Q)
                gather_time(u)
                forward_time(it, u)
                return 0

            lax.fori_loop(0, Q, both_step, 0)

        model = partial[it, q]
        for u in plane_from:
            part_copy(it, u, q).wait_recv()
            model = model + part_in[it, u]
        res[it, q] = weight * (model - vis_ref[...])
        for to in plane_next:
            res_copy(it, q, to).start()
        acc[...] = jnp.zeros_like(acc)

        def backward_step(i, _):
            backward_time(it, lax.rem(q - i + Q, Q))
            return 0

        lax.fori_loop(0, Q, backward_step, 0)

        for v in range(Z):
            for d in range(nd):
                for k in range(lane_tiles):
                    gout[it, v, :, d * S + k * 128:d * S + (k + 1) * 128] = acc[k, pl.ds(v * nd + d, 8, stride=D), :]
        for v in column_others:
            go_copy(it, z, v).start()
        grad = gout[it, z]
        for v in column_others:
            go_copy(it, v, z).wait_recv()
            grad = grad + gin[it, v]
        descent = grad + du[fi] + rho[...] * (jn[fi] - fit[fi])
        de[it, fi] = descent
        squares = descent * descent
        total = squares[:, 0:128]
        for lo in range(128, L, 128):
            total = total + squares[:, lo:lo + 128]
        sq[it, fi * T + me] = total
        each_other(lambda d: sq_copy(it, d // T, lax.rem(d, T)).start())
        last = it + 1 == ITERS
        if not last:
            for v in column_others:
                zd_copy(it, z, v).start()
        for f in freq_others:
            de_copy(it, fi, f).start()
        sq_all(it).wait_recv()
        for f in freq_others:
            de_copy(it, f, fi).wait_recv()
        if it == 0:
            for f in freq_others:
                state_copy(0, fi, f).wait_send()
                state_copy(1, fi, f).wait_send()
            for v in column_others:
                gz_copy(z, v).wait_send()
        scales = []
        for f in range(F):
            tile = jnp.sum(sq[it, pl.ds(f * T, T)], axis=0)
            whole = jnp.sum(jnp.sum(tile, axis=1, keepdims=True), axis=0, keepdims=True)
            scale = jnp.sqrt(whole / (8.0 * K * S) + epsilon)
            scales.append(scale)
            jn[f] = jn[f] - step_size * de[it, f] / scale
        consensus()
        for f in range(F):
            du[f] = du[f] + rho[...] * (jn[f] - fit[f])
        if not last:
            own = scales[0]
            for f in range(1, F):
                own = jnp.where(fi == f, scales[f], own)
            gz[z] = jn[fi]
            for v in column_others:
                zd_copy(it, v, z).wait_recv()
                gz[v] = gz[v] - step_size * zde[it, v] / own

    jones_out[...] = jn[fi]
    dual_out[...] = du[fi]
    for to in plane_next:
        st_copy(q, to).wait_send()
        coh_copy(q, to).wait_send()
        for it in range(ITERS):
            part_copy(it, q, to).wait_send()
            res_copy(it, q, to).wait_send()
    for it in range(ITERS):
        for v in column_others:
            go_copy(it, z, v).wait_send()
            if it + 1 < ITERS:
                zd_copy(it, z, v).wait_send()
        sq_all(it).wait_send()
        for f in freq_others:
            de_copy(it, fi, f).wait_send()


def body(visibilities, coherency, stations, jones, dual, cluster, rho_table):
    T = lax.axis_size("tm")
    F = lax.axis_size("freq")
    K, N = coherency.shape[3], coherency.shape[4]
    L = jones.shape[2]
    nd = K // T
    S = L // nd
    Z = math.gcd(T, 4)
    Q = T // Z
    D = Z * nd
    basis = poly_basis(F, min(3, F - 1))
    degrees = basis.shape[1]
    weight = np.float32(math.sqrt(S / (2.0 * T * N)))
    vmem = pl.BlockSpec(memory_space=pltpu.VMEM)
    smem = pl.BlockSpec(memory_space=pltpu.SMEM)
    anywhere = pl.BlockSpec(memory_space=pl.ANY)
    f32, bf16 = jnp.float32, jnp.bfloat16
    dma = pltpu.SemaphoreType.DMA
    jones_out, dual_out, poly = pl.pallas_call(
        functools.partial(kernel, T, F, Z, nd, S, K, N, basis, weight),
        out_shape=(
            jax.ShapeDtypeStruct((8, L), f32),
            jax.ShapeDtypeStruct((8, L), f32),
            jax.ShapeDtypeStruct((degrees, 8, L), f32),
        ),
        in_specs=[vmem, anywhere, vmem, vmem, vmem, smem, smem],
        out_specs=(vmem, vmem, vmem),
        scratch_shapes=[
            pltpu.VMEM((8, K, N), bf16),
            pltpu.VMEM((Q, 8 * D, N), bf16),
            pltpu.VMEM((Q, 8 * D, N), bf16),
            pltpu.VMEM((Q, 2, N), jnp.int32),
            pltpu.VMEM((Q, 2, S, N), bf16),
            pltpu.VMEM((2, 8 * D, S), bf16),
            pltpu.VMEM((2, S // 128, 8 * D, 128), f32),
            pltpu.VMEM((Z, 8, L), f32),
            pltpu.VMEM((ITERS, Z, 8, L), f32),
            pltpu.VMEM((Q, 2, 8 * D, N), f32),
            pltpu.VMEM((Q, 8 * D, N), f32),
            pltpu.VMEM((2, 2, 8 * D, N), bf16),
            pltpu.VMEM((ITERS, Q, 8, N), f32),
            pltpu.VMEM((ITERS, Q, 8, N), f32),
            pltpu.VMEM((ITERS, Q, 8, N), f32),
            pltpu.VMEM((S // 128, 8 * D, 128), f32),
            pltpu.VMEM((ITERS, Z, 8, L), f32),
            pltpu.VMEM((ITERS, Z, 8, L), f32),
            pltpu.VMEM((F, 8, L), f32),
            pltpu.VMEM((F, 8, L), f32),
            pltpu.VMEM((ITERS, F, 8, L), f32),
            pltpu.VMEM((F, 8, L), f32),
            pltpu.VMEM((8, L), f32),
            pltpu.VMEM((ITERS, F * T, 8, 128), f32),
            dma, dma((Q,)), dma((Q,)), dma((Q,)), dma((Q,)), dma((Z,)), dma((Z,)),
            dma((ITERS, Z)), dma((ITERS, Z)), dma((ITERS, Q)), dma((ITERS, Q)), dma((ITERS, Q)), dma((ITERS, Q)),
            dma((ITERS, Z)), dma((ITERS, Z)),
            dma((2, F)), dma((2, F)), dma((ITERS, F)), dma((ITERS, F)), dma((ITERS,)), dma((ITERS,)),
        ],
        compiler_params=pltpu.CompilerParams(
            collective_id=0, has_side_effects=True, vmem_limit_bytes=48 * 1024 * 1024),
        cost_estimate=pl.CostEstimate(flops=10**10, bytes_accessed=10**7, transcendentals=0),
    )(visibilities[0, 0], coherency[0, 0], stations[0], jones[0], dual[0], cluster, rho_table)
    return jones_out[None], dual_out[None], poly


def solution(mesh):
    return jax.shard_map(
        body,
        mesh=mesh,
        in_specs=(
            P("tm", "freq", None, None),
            P("tm", "freq", None, None, None),
            P("tm", None, None),
            P("freq", None, "tm"),
            P("freq", None, "tm"),
            P(),
            P(),
        ),
        out_specs=(P("freq", None, "tm"), P("freq", None, "tm"), P(None, None, "tm")),
        check_vma=False,
    )
```

time: 83.2 us -> 69.7 us (0.84)
  Pallas kernels: 76.9 us -> 62.7 us
    pallas_call x1, Pallas kernels: 76.9 us -> 62.7 us  [body(): pl.pallas_call(functools.partial(kernel, T, F, Z, nd, S, K, N, basis, wei...]
    unnamed x7 -> x17, local copies, waits for them, and re-layouts: 3 us -> 6 us
    another operation x2 -> x0, local copies, waits for them, and re-layouts: 1.4 us -> none  [body(): coherency[0, 0].reshape(8, T, nd, N).transpose(1, 0, 2, 3)]
    reshape x1 -> x0, local copies, waits for them, and re-layouts: 0.92 us -> none  [body(): coherency[0, 0].reshape(8, T, nd, N).transpose(1, 0, 2, 3)]
where the time goes in v2:
time: 69.7 us; the launch traced here: 69.4 us
  Pallas kernels  62.7 us (90%)
  local copies, waits for them, and re-layouts  6 us (9%)
    pallas_call x1, Pallas kernels, body(): pl.pallas_call(functools.partial(kernel, T, F, Z, nd, S, K, N, basis, wei...  62.7 us
    unnamed x17, local copies, waits for them, and re-layouts  6 us

profile of v2, /device:TPU:0, one launch (start us, length us, event | category | flops | bytes accessed | tf_op | source)
XLA Modules:
  0.0 69.4 jit_solution(3030815128539224077)
XLA Ops:
  0.6 0.0 copy-start.4
  0.6 0.0 copy-start.5
  0.7 0.0 copy-start.6
  0.7 0.7 copy-done.4
  1.3 0.0 copy-done.5
  1.3 0.0 copy-done.6
  1.3 0.0 copy-start
  1.3 1.0 %copy-done = bf16[1,1,8,64,512]{4,3,2,1,0:T(8,128)(2,1)S(1)} copy-done((bf16[1,1,8,64,512]{4,3,2,1,0:T(8,128)(2,1)S(1)}, bf16[1,1,8,64,512]{4,3,2,1,0:T(8,128)(2,1)}, u32[]{:S(2)}) %copy-start) | copy-done | bytes 524312
  2.4 0.0 copy-start.1
  2.4 0.8 %copy-done.1 = f32[1,8,2048]{2,1,0:T(8,128)S(1)} copy-done((f32[1,8,2048]{2,1,0:T(8,128)S(1)}, f32[1,8,2048]{2,1,0:T(8,128)}, u32[]{:S(2)}) %copy-start.1) | copy-done | bytes 65560
  3.2 0.0 copy-start.2
  3.2 0.8 %copy-done.2 = f32[1,8,2048]{2,1,0:T(8,128)S(1)} copy-done((f32[1,8,2048]{2,1,0:T(8,128)S(1)}, f32[1,8,2048]{2,1,0:T(8,128)}, u32[]{:S(2)}) %copy-start.2) | copy-done | bytes 65560
  4.0 0.0 copy-start.3
  4.1 0.7 %copy-done.3 = f32[1,1,8,512]{3,2,1,0:T(8,128)S(1)} copy-done((f32[1,1,8,512]{3,2,1,0:T(8,128)S(1)}, f32[1,1,8,512]{3,2,1,0:T(8,128)}, u32[]{:S(2)}) %copy-start.3) | copy-done | bytes 16408
  4.8 62.7 %shard_map.94 = (f32[8,2048]{1,0:T(8,128)S(1)}, f32[8,2048]{1,0:T(8,128)S(1)}, f32[1,8,2048]{2,1,0:T(8,128)S(1)}) custom-call(f32[8,512]{1,0:T(8,128)S(1)} %bitcast.12, bf16[8,64,512]{2,1,0:T(8,128)(2,1)S(1)} %bitcast.9, s32[2,512]{1,0:T(2,128)S(1)} %bitcast.13, f32[8,2048]{1,0:T(8,128)S(1)} %bitcast.10, f32[8,2048]{1,0:T(8,128)S(1)} %bitcast.11, ...), custom_call_target="tpu_custom_call" | custom-call | flops 10000000000 | bytes 10000000 | tf_op jit(solution)/shard_map/pallas_call | solution.py:437
  67.5 0.6 copy.13
  68.1 0.6 copy.14
  68.8 0.6 copy.15
Async XLA Ops:
  0.6 0.7 copy-start.4
  0.6 0.7 copy-start.5
  0.7 0.7 copy-start.6
  1.3 1.0 %copy-start = (bf16[1,1,8,64,512]{4,3,2,1,0:T(8,128)(2,1)S(1)}, bf16[1,1,8,64,512]{4,3,2,1,0:T(8,128)(2,1)}, u32[]{:S(2)}) copy-start(bf16[1,1,8,64,512]{4,3,2,1,0:T(8,128)(2,1)} %param.8) | copy-start | bytes 1572868
  2.4 0.8 %copy-start.1 = (f32[1,8,2048]{2,1,0:T(8,128)S(1)}, f32[1,8,2048]{2,1,0:T(8,128)}, u32[]{:S(2)}) copy-start(f32[1,8,2048]{2,1,0:T(8,128)} %param.10) | copy-start | bytes 196612
  3.2 0.8 %copy-start.2 = (f32[1,8,2048]{2,1,0:T(8,128)S(1)}, f32[1,8,2048]{2,1,0:T(8,128)}, u32[]{:S(2)}) copy-start(f32[1,8,2048]{2,1,0:T(8,128)} %param.11) | copy-start | bytes 196612
  4.0 0.7 %copy-start.3 = (f32[1,1,8,512]{3,2,1,0:T(8,128)S(1)}, f32[1,1,8,512]{3,2,1,0:T(8,128)}, u32[]{:S(2)}) copy-start(f32[1,1,8,512]{3,2,1,0:T(8,128)} %param.7) | copy-start | bytes 49156
